TPU v7x, 32 devices: a whole 2x2x4 slice. The times are simulated.
32 devices in a mesh: blk: 8 (over z, core), dp: 4 (over y, x).
Axes of the slice: x: 2, y: 2, z: 4, core: 2. Of those that a mesh axis runs over, the one named last changes fastest.
Arguments:
- queries: bfloat16 [64, 64, 1024], P(('dp', 'blk')), parts along dimension 0, may hold values from -8 to 8, as said below
- keys: bfloat16 [64, 64, 1024], P(('dp', 'blk')), parts along dimension 0, may hold values from -8 to 8, as said below
- values: bfloat16 [64, 64, 1024], P(('dp', 'blk')), parts along dimension 0, may hold values from -6 to 6
Outputs:
- attended: bfloat16 [64, 64, 1024], P(('dp', 'blk')), parts along dimension 0
There are 4 independent parts, one for each index of `dp`. A program takes and returns all parts, laid end to end along the dimension named above; each array names one. Nothing has to cross between parts.
Inputs may be any that keep to these rules, and one draw needn't show every extreme that they name: `queries`: queries of one pixel block. `keys`: keys of one pixel block.
All inputs are finite; a program needn't handle non-finite values.
Results may differ from a plain program's by a relative error of at most 0.0046.
Values may be sent and summed in bfloat16 or wider, within the bound.
A program may use at most 128 MiB of HBM per device.

v0:
```python
import jax
import jax.numpy as jnp
from jax import lax
from jax.sharding import PartitionSpec as P

HEADS = 8
HDIM = 128


def attend(carry, query_rows, query_band, key_rows, key_band, value_rows):
    running_max, denominator, weighted = carry
    scores = jnp.einsum(
        "qhd,khd->qhk", query_rows, key_rows, preferred_element_type=jnp.float32
    ) * HDIM ** (-0.5)
    keep = (query_band[:, None] >= key_band[None, :])[:, None, :]
    scores = jnp.where(keep, scores, jnp.float32(-1e30))
    new_max = jnp.maximum(running_max, jnp.max(scores, axis=2))
    weights = jnp.where(keep, jnp.exp(scores - new_max[:, :, None]), jnp.float32(0.0))
    denominator = jnp.sum(weights, axis=2)
    update = jnp.einsum(
        "qhk,khd->qhd", weights.astype(jnp.bfloat16), value_rows, preferred_element_type=jnp.float32
    )
    weighted = update
    return (new_max, denominator, weighted)


def empty_carry(row_count):
    return (
        jnp.full((row_count, HEADS), -1e30, jnp.float32),
        jnp.zeros((row_count, HEADS), jnp.float32),
        jnp.zeros((row_count, HEADS, HDIM), jnp.float32),
    )


def finish(carry):
    return (carry[2] / carry[1][:, :, None]).astype(jnp.bfloat16)


def shards(queries, keys, values):
    band_count, patch_count, width = queries.shape
    first_band = lax.axis_index("blk") * band_count
    row_count = band_count * patch_count
    query_rows = queries.reshape(row_count, HEADS, HDIM)
    query_band = first_band + jnp.arange(row_count, dtype=jnp.int32) // patch_count
    key_piece = lax.all_gather(keys, "blk", axis=0, tiled=True)
    value_piece = lax.all_gather(values, "blk", axis=0, tiled=True)
    piece_rows = key_piece.shape[0] * key_piece.shape[1]
    key_band = jnp.arange(piece_rows, dtype=jnp.int32) // key_piece.shape[1]

    def attend_piece(carry_in):
        return attend(
            carry_in,
            query_rows,
            query_band,
            key_piece.reshape(piece_rows, HEADS, HDIM),
            key_band,
            value_piece.reshape(piece_rows, HEADS, HDIM),
        )

    result = lax.cond(
        jnp.int32(0) <= first_band + band_count - 1,
        attend_piece,
        lambda carry_in: carry_in,
        empty_carry(row_count),
    )
    return finish(result).reshape(band_count, patch_count, width)


def solution(mesh):
    return jax.shard_map(
        shards,
        mesh=mesh,
        in_specs=(
            P(("dp", "blk"), None, None),
            P(("dp", "blk"), None, None),
            P(("dp", "blk"), None, None),
        ),
        out_specs=P(("dp", "blk"), None, None),
        check_vma=False,
    )
```

profile of v0, /device:TPU:0, one launch (start us, length us, event | category | flops | bytes accessed | tf_op | source)
XLA Modules:
  0.0 86.4 jit_solution(3563035082572923726)
XLA Ops:
  6.5 0.0 all-gather.3.cloned.1.call-start
  6.5 0.7 all-gather.3.cloned.1.call-update
  7.3 0.0 all-gather.5.cloned.1.call-start
  7.3 0.7 all-gather.5.cloned.1.call-update
  8.0 32.8 %all-gather.3.cloned.1.call-done = bf16[16,64,1024]{2,1,0:T(8,128)(2,1)} async-done(((bf16[2,64,1024]{2,1,0:T(8,128)(2,1)}), bf16[16,64,1024]{2,1,0:T(8,128)(2,1)}) %all-gather.3.cloned.1.call-update) | async-done | bytes 2097168 | tf_op jit(solution)/shard_map/all_gather | solution.py:45
  40.8 30.2 %all-gather.5.cloned.1.call-done = bf16[16,64,1024]{2,1,0:T(8,128)(2,1)} async-done(((bf16[2,64,1024]{2,1,0:T(8,128)(2,1)}), bf16[16,64,1024]{2,1,0:T(8,128)(2,1)}) %all-gather.5.cloned.1.call-update) | async-done | bytes 2097168 | tf_op jit(solution)/shard_map/all_gather | solution.py:46
  71.0 7.4 %conditional.1 = (f32[128,8]{0,1:T(8,128)S(1)}, f32[128,8,128]{2,0,1:T(8,128)S(1)}) conditional(s32[]{:T(128)} %convert_element_type.11, () %tuple.33, (s32[]{:T(128)}, s32[128]{0:T(128)S(1)}, s32[1024]{0:T(1024)S(1)}, bf16[16,64,1024]{2,1,0:T(8,128)(2,1)}, bf16[2,64,1024]{2,1,0:T(8,128)(2,1)}, /*index=5*/bf16[16,64,1024]{2,1,0:T(8,128)(2,1)}) %tuple.34), branch_computations={%region_0.1_spmd, %region_1.4_spmd} | conditional | flops 550641792 | bytes 36476492 | solution.py:60
  71.0 0.0 copy-start.1
  71.0 0.2 broadcast_compare_fusion
  71.3 2.2 %copy.17 = bf16[128,8,8,128]{3,2,1,0:T(8,128)(2,1)S(1)} copy(bf16[128,8,8,128]{3,1,2,0:T(8,128)(2,1)} %bitcast.24) | data formatting | bytes 4194304 | tf_op jit(solution)/shard_map/cond
  73.5 0.0 copy-start
  73.5 0.0 copy-done.1
  73.5 0.9 %fusion = (f32[128,8]{0,1:T(8,128)S(1)}, f32[8,1024,128]{2,1,0:T(8,128)S(1)}) fusion(pred[128,1024]{0,1:T(8,128)(4,1)S(1)} %broadcast_compare_fusion, bf16[128,8,128]{2,1,0:T(8,128)(2,1)S(1)} %bitcast.29, bf16[1024,8,128]{2,1,0:T(8,128)(2,1)S(1)} %bitcast.26), kind=kOutput, calls=%fused_computation.2 | convolution fusion | flops 271580160 | bytes 6688768 | tf_op jit(solution)/shard_map/cond/branch_1_fun/qhd,khd->qhk/dot_general | solution.py:12
  74.5 0.6 copy-done
  75.1 0.6 copy.19
  75.7 1.7 %fusion.13 = f32[128,8,128]{2,0,1:T(8,128)S(1)} fusion(bf16[1024,8,128]{2,1,0:T(8,128)(2,1)S(1)} %bitcast.27, f32[8,1024,128]{2,1,0:T(8,128)S(1)} %get-tuple-element.135, f32[128,8]{0,1:T(8,128)S(1)} %broadcast_maximum_fusion, pred[128,1024]{0,1:T(8,128)(4,1)S(1)} %broadcast_compare_fusion), kind=kOutput, calls=%fused_computation.14 | convolution fusion | flops 273678336 | bytes 6950912 | tf_op jit(solution)/shard_map/cond/branch_1_fun/qhk,khd->qhd/dot_general | solution.py:20
  77.4 1.0 %fusion.2 = f32[128,8]{0,1:T(8,128)S(1)} fusion(f32[8,1024,128]{2,1,0:T(8,128)S(1)} %get-tuple-element.135, f32[128,8]{0,1:T(8,128)S(1)} %broadcast_maximum_fusion, pred[128,1024]{0,1:T(8,128)(4,1)S(1)} %broadcast_compare_fusion), kind=kLoop, calls=%fused_computation.4 | loop fusion | flops 5241856 | bytes 4333568 | tf_op jit(solution)/shard_map/cond/branch_1_fun/reduce_sum | solution.py:19
  78.4 0.2 divide_convert_fusion
  78.6 0.2 copy.15
  78.8 0.8 reshape.46
  (6 shorter events, 0.1 us)
Async XLA Ops:
  6.5 34.3 %all-gather.3.cloned.1.call-start = ((), (), s32[]{:S(2)}) async-start(), calls=%async_computation | async-start | bytes 2359296 | tf_op jit(solution)/shard_map/all_gather | solution.py:45
  7.3 63.8 %all-gather.5.cloned.1.call-start = ((), (), s32[]{:S(2)}) async-start(), calls=%async_computation.1 | async-start | bytes 2359296 | tf_op jit(solution)/shard_map/all_gather | solution.py:46
  71.0 2.5 %copy-start.1 = (bf16[2,64,1024]{2,1,0:T(8,128)(2,1)S(1)}, bf16[2,64,1024]{2,1,0:T(8,128)(2,1)}, u32[]{:S(2)}) copy-start(bf16[2,64,1024]{2,1,0:T(8,128)(2,1)} %get-tuple-element.133) | copy-start | bytes 786436 | tf_op jit(solution)/shard_map/cond
  73.5 1.6 %copy-start = (bf16[16,64,1024]{2,1,0:T(8,128)(2,1)S(1)}, bf16[16,64,1024]{2,1,0:T(8,128)(2,1)}, u32[]{:S(2)}) copy-start(bf16[16,64,1024]{2,1,0:T(8,128)(2,1)} %get-tuple-element.127) | copy-start | bytes 6291460 | tf_op jit(solution)/shard_map/cond
Sparse Core Ops, SparseCore 0:
  9.0 31.7 all-gather.2
  42.4 28.5 all-gather.4
where the time goes:
time: 86.6 us; the launch traced here: 86.4 us
  waiting for transfers between devices  64.4 us (74%)
  between operations  13.4 us (15%)
  local copies, waits for them, and re-layouts  4.47 us (5%)
  matrix products  2.58 us (3%)
  other arithmetic  1.43 us (2%)
    all_gather x1, waiting for transfers between devices, shards(): key_piece = lax.all_gather(keys, 'blk', axis=0, tiled=True)  32.8 us
    all_gather x1, waiting for transfers between devices, shards(): value_piece = lax.all_gather(values, 'blk', axis=0, tiled=True)  30.2 us
    cond x7, local copies, waits for them, and re-layouts  3.47 us
  transfers between devices with their start and end apart: 2, of which 2 were waited for; matrix products, arithmetic and copies ran while one was open for 0% of the time, Pallas kernels for 0%

commit v1 on v0

v1 whole, which is shorter than its diff:
```python
import functools
import math

import jax
import jax.numpy as jnp
from jax import lax
from jax.experimental import pallas as pl
from jax.experimental.pallas import tpu as pltpu
from jax.sharding import PartitionSpec as P

HDIM = 128
MESH = pl.DeviceIdType.MESH
SCALE = HDIM ** (-0.5) * math.log2(math.e)


def softmax_block(q, k, v, keep=None):
    s = lax.dot_general(q, k, (((1,), (1,)), ((), ())), preferred_element_type=jnp.float32)
    if keep is not None:
        s = jnp.where(keep, s, jnp.float32(-1e30))
    top = jnp.max(s, axis=1, keepdims=True)
    p = jnp.exp2((s - top) * SCALE)
    p = p.astype(jnp.bfloat16)
    ve = jnp.concatenate([v, jnp.ones_like(v)], axis=1)
    o = jnp.dot(p, ve, preferred_element_type=jnp.float32)
    total = o[:, HDIM:]
    return o[:, :HDIM] / total, top * SCALE + jnp.log2(total)


def kernel(
    chips, patches,
    q_hbm, k_hbm, v_hbm, o_ref,
    q_v, k_v, v_v, sib_k, sib_v, kall, vall, qall, out_p, out_s, part, stat, loc_o, loc_s,
    load_sem, own_sem, kv_send, kv_recv, q_send, q_recv, sib_send, sib_recv, sibh_send, sibh_recv,
    part_send, part_recv,
):
    rows, width = q_v.shape
    heads = width // HDIM
    half = heads // 2
    mid = chips // 2
    hub = mid - 1
    me = lax.axis_index("blk")
    z, c = me // 2, me % 2
    other = 1 - c
    sib = z * 2 + other
    lower = z < mid
    base = jnp.where(lower, z * (2 * rows), 0)

    def remote(src, dst, send, recv, dev):
        return pltpu.make_async_remote_copy(
            src_ref=src, dst_ref=dst, send_sem=send, recv_sem=recv,
            device_id={"blk": dev}, device_id_type=MESH,
        )

    def lanes(h):
        return pl.ds(pl.multiple_of(h * HDIM, HDIM), HDIM)

    def span(at, count=1):
        return pl.ds(pl.multiple_of(at, rows), count * rows)

    def each(lo, hi, body):
        def step(i, carry):
            body(i)
            return carry
        lax.fori_loop(lo, hi, step, 0)

    loads = [
        pltpu.make_async_copy(src, dst, load_sem.at[n])
        for n, (src, dst) in enumerate(((q_hbm, q_v), (k_hbm, k_v), (v_hbm, v_v)))
    ]
    for copy in loads:
        copy.start()
    own = []
    for h in range(half):
        at = lanes(c * half + h)
        own.append((
            pltpu.make_async_copy(k_hbm.at[:, at], kall.at[h, span(base + c * rows)], own_sem.at[h, 0]),
            pltpu.make_async_copy(v_hbm.at[:, at], vall.at[h, span(base + c * rows)], own_sem.at[h, 1]),
            pltpu.make_async_copy(q_hbm.at[:, at], qall.at[h, span((mid * 2 + c) * rows)], own_sem.at[h, 2]),
        ))
        for copy in own[-1]:
            copy.start()

    barrier = pltpu.get_barrier_semaphore()
    count = 2 * chips
    for step in range(1, count):
        pl.semaphore_signal(
            barrier, inc=1, device_id={"blk": lax.rem(me + step, count)}, device_id_type=MESH
        )
    pl.semaphore_wait(barrier, count - 1)
    for copy in loads:
        copy.wait()

    def kv_push(h, do):
        def to(j):
            for cc in range(2):
                at = lanes(cc * half + h)
                for n, (src, dst) in enumerate(((k_v, kall), (v_v, vall))):
                    do(remote(src.at[:, at], dst.at[h, span((z * 2 + c) * rows)],
                              kv_send.at[j, cc, h, n], kv_recv.at[z, c, h, n], j * 2 + cc))
        each(z + 1, jnp.where(lower, mid, 0), to)

    def q_push(h, do):
        def to(i):
            for cc in range(2):
                do(remote(q_v.at[:, lanes(cc * half + h)], qall.at[h, span(((z - mid) * 2 + c) * rows)],
                          q_send.at[i - hub, cc, h], q_recv.at[z - mid, c, h], i * 2 + cc))
        each(hub, jnp.where(lower, 0, z), to)

    def sib_push(h, do):
        at = lanes(other * half + h)
        for n, (src, dst, row) in enumerate((
            (k_v, kall, base + c * rows), (v_v, vall, base + c * rows), (q_v, qall, (mid * 2 + c) * rows),
        )):
            do(remote(src.at[:, at], dst.at[h, span(row)], sibh_send.at[h, n], sibh_recv.at[h, n], sib))

    def sib_whole(do):
        @pl.when(c == 0)
        def _():
            for n, (src, dst) in enumerate(((k_v, sib_k), (v_v, sib_v))):
                do(remote(src, dst, sib_send.at[n], sib_recv.at[n], sib))

    def start(copy):
        copy.start()

    def wait_send(copy):
        copy.wait_send()

    for h in range(half):
        kv_push(h, start)
        q_push(h, start)
        if h == 0:
            sib_whole(start)
        sib_push(h, start)

    row_band = lax.broadcasted_iota(jnp.int32, (rows, rows), 0) // patches
    key_band = lax.broadcasted_iota(jnp.int32, (rows, rows), 1) // patches
    keep = row_band >= key_band

    @pl.when(c == 0)
    def _():
        def body(h):
            at = lanes(h)
            loc_o[h], loc_s[h] = softmax_block(q_v[:, at], k_v[:, at], v_v[:, at], keep)
        each(0, heads, body)

    @pl.when(c == 1)
    def _():
        for n, dst in enumerate((sib_k, sib_v)):
            remote(dst, dst, sib_send.at[n], sib_recv.at[n], sib).wait_recv()
        keep2 = jnp.concatenate([keep, jnp.full((rows, rows), True)], axis=1)

        def body(h):
            at = lanes(h)
            loc_o[h], loc_s[h] = softmax_block(
                q_v[:, at],
                jnp.concatenate([k_v[:, at], sib_k[:, at]], axis=0),
                jnp.concatenate([v_v[:, at], sib_v[:, at]], axis=0),
                keep2,
            )
        each(0, heads, body)

    def block(q_slot, h, key_at, key_count):
        q = qall[h, span(q_slot * 2 * rows, 2), :]
        o, s = softmax_block(q, kall[h, key_at : key_at + key_count, :] if isinstance(key_at, int)
                             else kall[h, pl.ds(pl.multiple_of(key_at, rows), key_count), :],
                             vall[h, key_at : key_at + key_count, :] if isinstance(key_at, int)
                             else vall[h, pl.ds(pl.multiple_of(key_at, rows), key_count), :])
        return o.astype(jnp.bfloat16), s.T[0:1, :]

    def deliver(q_slot, h, slot, chip, cc, do):
        for n, (src, dst) in enumerate(((out_p, part), (out_s, stat))):
            do(remote(src.at[q_slot, cc, h], dst.at[slot, c * half + h],
                      part_send.at[q_slot, cc, h, n], part_recv.at[slot, c * half + h, n], chip * 2 + cc))

    def compute(q_slot, h, key_at, key_count, slot, chip):
        o, s = block(q_slot, h, key_at, key_count)
        for cc in range(2):
            out_p[q_slot, cc, h] = o[cc * rows : (cc + 1) * rows]
            out_s[q_slot, cc, h] = s[:, cc * rows : (cc + 1) * rows]
            deliver(q_slot, h, slot, chip, cc, start)

    def wait_local_kv(h):
        for n in range(2):
            own[h][n].wait()
        for n, dst in enumerate((kall, vall)):
            ref = dst.at[h, span(base + other * rows)]
            remote(ref, ref, sibh_send.at[h, n], sibh_recv.at[h, n], sib).wait_recv()

    def wait_own_q(h):
        own[h][2].wait()
        ref = qall.at[h, span((mid * 2 + other) * rows)]
        remote(ref, ref, sibh_send.at[h, 2], sibh_recv.at[h, 2], sib).wait_recv()

    def wait_q(j, h):
        for cc in range(2):
            ref = qall.at[h, span(((j - mid) * 2 + cc) * rows)]
            remote(ref, ref, q_send.at[0, cc, h], q_recv.at[j - mid, cc, h], sib).wait_recv()

    def wait_kv(i, h):
        for cc in range(2):
            for n, dst in enumerate((kall, vall)):
                ref = dst.at[h, span((i * 2 + cc) * rows)]
                remote(ref, ref, kv_send.at[0, cc, h, n], kv_recv.at[i, cc, h, n], sib).wait_recv()

    for h in range(half):
        wait_local_kv(h)
        wait_own_q(h)

        @pl.when(lower)
        def _():
            each(0, z, lambda i: wait_kv(i, h))

            @pl.when(z == hub)
            def _():
                def body(n):
                    j = chips - 1 - n
                    wait_q(j, h)
                    compute(j - mid, h, 0, 2 * mid * rows, 0, j)
                each(0, chips - mid, body)

            def body(i):
                o, s = block(mid, h, i * 2 * rows, 2 * rows)
                for cc in range(2):
                    @pl.when(cc == c)
                    def _():
                        part[i, c * half + h] = o[cc * rows : (cc + 1) * rows]
                        stat[i, c * half + h] = s[:, cc * rows : (cc + 1) * rows]

                    @pl.when(cc != c)
                    def _():
                        out_p[mid + i, cc, h] = o[cc * rows : (cc + 1) * rows]
                        out_s[mid + i, cc, h] = s[:, cc * rows : (cc + 1) * rows]
                        deliver(mid + i, h, i, z, cc, start)
            each(0, z, body)

        @pl.when(jnp.logical_not(lower))
        def _():
            def body(j):
                wait_q(j, h)
                compute(j - mid, h, 0, 2 * rows, 1 + z - mid, j)
            each(z + 1, chips, body)

    def finish(head, from_me):
        at = lanes(head)

        def merge(slot, carry):
            acc, weight, top = carry
            @pl.when(jnp.logical_not(jnp.logical_and(lower, from_me)))
            def _():
                for n, dst in enumerate((part, stat)):
                    ref = dst.at[slot, head]
                    remote(ref, ref, part_send.at[0, 0, 0, n], part_recv.at[slot, head, n], sib).wait_recv()
            s = jnp.broadcast_to(stat[slot, head], (HDIM, rows)).T
            new_top = jnp.maximum(top, s)
            a, b = jnp.exp2(top - new_top), jnp.exp2(s - new_top)
            return acc * a + part[slot, head].astype(jnp.float32) * b, weight * a + b, new_top

        acc, weight, _ = lax.fori_loop(
            0, jnp.where(lower, z, z - mid + 1), merge,
            (loc_o[head], jnp.ones((rows, HDIM), jnp.float32), loc_s[head]),
        )
        o_ref[:, at] = (acc / weight).astype(o_ref.dtype)

    for h in range(half):
        for cc in range(2):
            finish(cc * half + h, cc == c)

    for h in range(half):
        kv_push(h, wait_send)
        q_push(h, wait_send)
        sib_push(h, wait_send)

        @pl.when(z == hub)
        def _():
            def body(j):
                for cc in range(2):
                    deliver(j - mid, h, 0, j, cc, wait_send)
            each(mid, chips, body)

        @pl.when(lower)
        def _():
            each(0, z, lambda i: deliver(mid + i, h, i, z, other, wait_send))

        @pl.when(jnp.logical_not(lower))
        def _():
            def body(j):
                for cc in range(2):
                    deliver(j - mid, h, 1 + z - mid, j, cc, wait_send)
            each(z + 1, chips, body)
    sib_whole(wait_send)


def shards(chips, queries, keys, values):
    band_count, patch_count, width = queries.shape
    rows = band_count * patch_count
    heads = width // HDIM
    half = heads // 2
    mid = chips // 2
    bf16, f32 = jnp.bfloat16, jnp.float32
    dma = pltpu.SemaphoreType.DMA
    out = pl.pallas_call(
        functools.partial(kernel, chips, patch_count),
        out_shape=jax.ShapeDtypeStruct((rows, width), bf16),
        in_specs=[pl.BlockSpec(memory_space=pl.ANY)] * 3,
        out_specs=pl.BlockSpec(memory_space=pltpu.VMEM),
        scratch_shapes=[
            pltpu.VMEM((rows, width), bf16),
            pltpu.VMEM((rows, width), bf16),
            pltpu.VMEM((rows, width), bf16),
            pltpu.VMEM((rows, width), bf16),
            pltpu.VMEM((rows, width), bf16),
            pltpu.VMEM((half, 2 * mid * rows, HDIM), bf16),
            pltpu.VMEM((half, 2 * mid * rows, HDIM), bf16),
            pltpu.VMEM((half, 2 * (mid + 1) * rows, HDIM), bf16),
            pltpu.VMEM((2 * mid, 2, half, rows, HDIM), bf16),
            pltpu.VMEM((2 * mid, 2, half, 1, rows), f32),
            pltpu.VMEM((mid, heads, rows, HDIM), bf16),
            pltpu.VMEM((mid, heads, 1, rows), f32),
            pltpu.VMEM((heads, rows, HDIM), f32),
            pltpu.VMEM((heads, rows, HDIM), f32),
            dma((3,)),
            dma((half, 3)),
            dma((mid, 2, half, 2)),
            dma((mid, 2, half, 2)),
            dma((mid, 2, half)),
            dma((mid, 2, half)),
            dma((2,)),
            dma((2,)),
            dma((half, 3)),
            dma((half, 3)),
            dma((2 * mid, 2, half, 2)),
            dma((mid, heads, 2)),
        ],
        compiler_params=pltpu.CompilerParams(
            collective_id=0, has_side_effects=True, vmem_limit_bytes=48 * 1024 * 1024
        ),
        cost_estimate=pl.CostEstimate(
            flops=4 * rows * chips * rows * width, bytes_accessed=8 * rows * width, transcendentals=0
        ),
    )(*(a.reshape(rows, width) for a in (queries, keys, values)))
    return out.reshape(band_count, patch_count, width)


def solution(mesh):
    spec = P(("dp", "blk"), None, None)
    return jax.shard_map(
        functools.partial(shards, mesh.shape["blk"] // 2),
        mesh=mesh,
        in_specs=(spec, spec, spec),
        out_specs=spec,
        check_vma=False,
    )
```

time: 86.6 us -> 27.4 us (0.32)
  the two profiles are of different devices: /device:TPU:0 before, /device:TPU:21 now
where the time goes in v1:
time: 27.4 us; the launch traced here: 27.2 us
  Pallas kernels  23.6 us (86%)
  local copies, waits for them, and re-layouts  3.55 us (13%)
    pallas_call x1, Pallas kernels, shards(): pl.pallas_call(functools.partial(kernel, chips, patch_count), out_shape=j...  23.6 us
    unnamed x7, local copies, waits for them, and re-layouts  3.55 us

profile of v1, /device:TPU:21, one launch (start us, length us, event | category | flops | bytes accessed | tf_op | source)
XLA Modules:
  0.0 27.2 jit_solution(18002981899290317823)
XLA Ops:
  0.0 0.0 copy-start
  0.0 0.9 %copy-done = bf16[2,64,1024]{2,1,0:T(8,128)(2,1)S(1)} copy-done((bf16[2,64,1024]{2,1,0:T(8,128)(2,1)S(1)}, bf16[2,64,1024]{2,1,0:T(8,128)(2,1)}, u32[]{:S(2)}) %copy-start) | copy-done | bytes 262168
  1.0 0.0 copy-start.1
  1.0 0.9 %copy-done.1 = bf16[2,64,1024]{2,1,0:T(8,128)(2,1)S(1)} copy-done((bf16[2,64,1024]{2,1,0:T(8,128)(2,1)S(1)}, bf16[2,64,1024]{2,1,0:T(8,128)(2,1)}, u32[]{:S(2)}) %copy-start.1) | copy-done | bytes 262168
  1.9 0.0 copy-start.2
  1.9 0.9 %copy-done.2 = bf16[2,64,1024]{2,1,0:T(8,128)(2,1)S(1)} copy-done((bf16[2,64,1024]{2,1,0:T(8,128)(2,1)S(1)}, bf16[2,64,1024]{2,1,0:T(8,128)(2,1)}, u32[]{:S(2)}) %copy-start.2) | copy-done | bytes 262168
  2.9 23.6 %shard_map.37 = bf16[128,1024]{1,0:T(8,128)(2,1)S(1)} custom-call(bf16[128,1024]{1,0:T(8,128)(2,1)S(1)} %bitcast.5, bf16[128,1024]{1,0:T(8,128)(2,1)S(1)} %bitcast.6, bf16[128,1024]{1,0:T(8,128)(2,1)S(1)} %bitcast.7), custom_call_target="tpu_custom_call" | custom-call | flops 268435456 | bytes 1048576 | tf_op jit(solution)/shard_map/pallas_call | solution.py:301
  26.5 0.7 %copy.5 = bf16[2,64,1024]{2,1,0:T(8,128)(2,1)} copy(bf16[2,64,1024]{2,1,0:T(8,128)(2,1)S(1)} %bitcast.4) | data formatting | bytes 524288
Async XLA Ops:
  0.0 0.9 %copy-start = (bf16[2,64,1024]{2,1,0:T(8,128)(2,1)S(1)}, bf16[2,64,1024]{2,1,0:T(8,128)(2,1)}, u32[]{:S(2)}) copy-start(bf16[2,64,1024]{2,1,0:T(8,128)(2,1)} %param.3) | copy-start | bytes 786436
  1.0 0.9 %copy-start.1 = (bf16[2,64,1024]{2,1,0:T(8,128)(2,1)S(1)}, bf16[2,64,1024]{2,1,0:T(8,128)(2,1)}, u32[]{:S(2)}) copy-start(bf16[2,64,1024]{2,1,0:T(8,128)(2,1)} %param.4) | copy-start | bytes 786436
  1.9 0.9 %copy-start.2 = (bf16[2,64,1024]{2,1,0:T(8,128)(2,1)S(1)}, bf16[2,64,1024]{2,1,0:T(8,128)(2,1)}, u32[]{:S(2)}) copy-start(bf16[2,64,1024]{2,1,0:T(8,128)(2,1)} %param.5) | copy-start | bytes 786436

commit v2 on v1

--- a/solution.py
+++ b/solution.py
@@ -10,6 +10,7 @@
 
 HDIM = 128
 MESH = pl.DeviceIdType.MESH
+WINDOW = 3
 SCALE = HDIM ** (-0.5) * math.log2(math.e)
 
 
@@ -28,10 +29,10 @@
 
 def kernel(
     chips, patches,
-    q_hbm, k_hbm, v_hbm, o_ref,
-    q_v, k_v, v_v, sib_k, sib_v, kall, vall, qall, out_p, out_s, part, stat, loc_o, loc_s,
+    q_hbm, k_hbm, v_hbm, o_hbm,
+    o_v, q_v, k_v, v_v, sib_k, sib_v, kall, vall, qall, out_p, out_s, part, stat, loc_o, loc_s,
     load_sem, own_sem, kv_send, kv_recv, q_send, q_recv, sib_send, sib_recv, sibh_send, sibh_recv,
-    part_send, part_recv,
+    part_send, part_recv, out_sem,
 ):
     rows, width = q_v.shape
     heads = width // HDIM
@@ -83,28 +84,34 @@
     barrier = pltpu.get_barrier_semaphore()
     count = 2 * chips
     for step in range(1, count):
-        pl.semaphore_signal(
-            barrier, inc=1, device_id={"blk": lax.rem(me + step, count)}, device_id_type=MESH
-        )
-    pl.semaphore_wait(barrier, count - 1)
-    for copy in loads:
-        copy.wait()
-
-    def kv_push(h, do):
+        dev = lax.rem(me + step, count)
+        y = dev // 2
+
+        @pl.when((lower & (y < mid)) | ((z >= mid) & (y >= mid)) | (z == hub) | (y == hub))
+        def _():
+            pl.semaphore_signal(barrier, inc=1, device_id={"blk": dev}, device_id_type=MESH)
+    pl.semaphore_wait(barrier, jnp.where(
+        z == hub, count - 1, jnp.where(lower, 2 * mid - 1, 2 * (chips - mid) + 1)
+    ))
+
+    def kv_push(h, cc, do):
         def to(j):
-            for cc in range(2):
-                at = lanes(cc * half + h)
-                for n, (src, dst) in enumerate(((k_v, kall), (v_v, vall))):
-                    do(remote(src.at[:, at], dst.at[h, span((z * 2 + c) * rows)],
-                              kv_send.at[j, cc, h, n], kv_recv.at[z, c, h, n], j * 2 + cc))
+            at = lanes(cc * half + h)
+            for n, (src, dst) in enumerate(((k_hbm, kall), (v_hbm, vall))):
+                do(remote(src.at[:, at], dst.at[h, span((z * 2 + c) * rows)],
+                          kv_send.at[j, cc, h, n], kv_recv.at[z, c, h, n], j * 2 + cc))
         each(z + 1, jnp.where(lower, mid, 0), to)
 
-    def q_push(h, do):
+    def q_push(h, cc, do):
         def to(i):
-            for cc in range(2):
-                do(remote(q_v.at[:, lanes(cc * half + h)], qall.at[h, span(((z - mid) * 2 + c) * rows)],
-                          q_send.at[i - hub, cc, h], q_recv.at[z - mid, c, h], i * 2 + cc))
+            do(remote(q_hbm.at[:, lanes(cc * half + h)], qall.at[h, span(((z - mid) * 2 + c) * rows)],
+                      q_send.at[i - hub, cc, h], q_recv.at[z - mid, c, h], i * 2 + cc))
         each(hub, jnp.where(lower, 0, z), to)
+
+    def push(item, do):
+        h, cc = item // 2, item % 2
+        kv_push(h, cc, do)
+        q_push(h, cc, do)
 
     def sib_push(h, do):
         at = lanes(other * half + h)
@@ -125,39 +132,40 @@
     def wait_send(copy):
         copy.wait_send()
 
-    for h in range(half):
-        kv_push(h, start)
-        q_push(h, start)
-        if h == 0:
-            sib_whole(start)
+    for item in range(min(WINDOW, heads)):
+        push(item, start)
+    for copy in loads:
+        copy.wait()
+    sib_whole(start)
+    for h in range(half):
         sib_push(h, start)
 
     row_band = lax.broadcasted_iota(jnp.int32, (rows, rows), 0) // patches
     key_band = lax.broadcasted_iota(jnp.int32, (rows, rows), 1) // patches
     keep = row_band >= key_band
 
-    @pl.when(c == 0)
-    def _():
-        def body(h):
-            at = lanes(h)
-            loc_o[h], loc_s[h] = softmax_block(q_v[:, at], k_v[:, at], v_v[:, at], keep)
-        each(0, heads, body)
+    keep2 = jnp.concatenate([keep, jnp.full((rows, rows), True)], axis=1)
 
     @pl.when(c == 1)
     def _():
         for n, dst in enumerate((sib_k, sib_v)):
             remote(dst, dst, sib_send.at[n], sib_recv.at[n], sib).wait_recv()
-        keep2 = jnp.concatenate([keep, jnp.full((rows, rows), True)], axis=1)
-
-        def body(h):
-            at = lanes(h)
+
+    def attend_local(h):
+        at = lanes(h)
+
+        @pl.when(c == 0)
+        def _():
+            loc_o[h], loc_s[h] = softmax_block(q_v[:, at], k_v[:, at], v_v[:, at], keep)
+
+        @pl.when(c == 1)
+        def _():
             loc_o[h], loc_s[h] = softmax_block(
                 q_v[:, at],
                 jnp.concatenate([k_v[:, at], sib_k[:, at]], axis=0),
                 jnp.concatenate([v_v[:, at], sib_v[:, at]], axis=0),
                 keep2,
             )
-        each(0, heads, body)
 
     def block(q_slot, h, key_at, key_count):
         q = qall[h, span(q_slot * 2 * rows, 2), :]
@@ -202,10 +210,24 @@
                 ref = dst.at[h, span((i * 2 + cc) * rows)]
                 remote(ref, ref, kv_send.at[0, cc, h, n], kv_recv.at[i, cc, h, n], sib).wait_recv()
 
-    for h in range(half):
-        wait_local_kv(h)
-        wait_own_q(h)
-
+    for item in range(heads):
+        h = item // 2
+        attend_local(item)
+        if item + WINDOW < heads:
+            push(item, wait_send)
+            push(item + WINDOW, start)
+        if item % 2 == 1:
+            wait_local_kv(h)
+            wait_own_q(h)
+
+            @pl.when(jnp.logical_not(lower))
+            def _():
+                def body(j):
+                    wait_q(j, h)
+                    compute(j - mid, h, 0, 2 * rows, 1 + z - mid, j)
+                each(z + 1, chips, body)
+
+    for h in range(half):
         @pl.when(lower)
         def _():
             each(0, z, lambda i: wait_kv(i, h))
@@ -233,12 +255,9 @@
                         deliver(mid + i, h, i, z, cc, start)
             each(0, z, body)
 
-        @pl.when(jnp.logical_not(lower))
-        def _():
-            def body(j):
-                wait_q(j, h)
-                compute(j - mid, h, 0, 2 * rows, 1 + z - mid, j)
-            each(z + 1, chips, body)
+    def out_copy(head):
+        at = lanes(head)
+        return pltpu.make_async_copy(o_v.at[:, at], o_hbm.at[:, at], out_sem.at[head])
 
     def finish(head, from_me):
         at = lanes(head)
@@ -259,15 +278,18 @@
             0, jnp.where(lower, z, z - mid + 1), merge,
             (loc_o[head], jnp.ones((rows, HDIM), jnp.float32), loc_s[head]),
         )
-        o_ref[:, at] = (acc / weight).astype(o_ref.dtype)
+        o_v[:, at] = (acc / weight).astype(o_v.dtype)
+        out_copy(head).start()
 
     for h in range(half):
         for cc in range(2):
             finish(cc * half + h, cc == c)
 
-    for h in range(half):
-        kv_push(h, wait_send)
-        q_push(h, wait_send)
+    for item in range(max(heads - WINDOW, 0), heads):
+        push(item, wait_send)
+    for head in range(heads):
+        out_copy(head).wait()
+    for h in range(half):
         sib_push(h, wait_send)
 
         @pl.when(z == hub)
@@ -302,8 +324,9 @@
         functools.partial(kernel, chips, patch_count),
         out_shape=jax.ShapeDtypeStruct((rows, width), bf16),
         in_specs=[pl.BlockSpec(memory_space=pl.ANY)] * 3,
-        out_specs=pl.BlockSpec(memory_space=pltpu.VMEM),
+        out_specs=pl.BlockSpec(memory_space=pl.ANY),
         scratch_shapes=[
+            pltpu.VMEM((rows, width), bf16),
             pltpu.VMEM((rows, width), bf16),
             pltpu.VMEM((rows, width), bf16),
             pltpu.VMEM((rows, width), bf16),
@@ -330,9 +353,10 @@
             dma((half, 3)),
             dma((2 * mid, 2, half, 2)),
             dma((mid, heads, 2)),
+            dma((heads,)),
         ],
         compiler_params=pltpu.CompilerParams(
-            collective_id=0, has_side_effects=True, vmem_limit_bytes=48 * 1024 * 1024
+            collective_id=0, has_side_effects=True, vmem_limit_bytes=62 * 1024 * 1024
         ),
         cost_estimate=pl.CostEstimate(
             flops=4 * rows * chips * rows * width, bytes_accessed=8 * rows * width, transcendentals=0

time: 27.4 us -> 24.9 us (0.909)
  local copies, waits for them, and re-layouts: 3.55 us -> 1.67 us
  Pallas kernels: 23.6 us -> 23.1 us
    unnamed x7 -> x1, local copies, waits for them, and re-layouts: 3.55 us -> 1.67 us
    pallas_call x1, Pallas kernels: 23.6 us -> 23.1 us  [shards(): pl.pallas_call(functools.partial(kernel, chips, patch_count), out_shape=j...]
where the time goes in v2:
time: 24.9 us; the launch traced here: 24.8 us
  Pallas kernels  23.1 us (93%)
  local copies, waits for them, and re-layouts  1.67 us (7%)
    pallas_call x1, Pallas kernels, shards(): pl.pallas_call(functools.partial(kernel, chips, patch_count), out_shape=j...  23.1 us
    unnamed x1, local copies, waits for them, and re-layouts  1.67 us

profile of v2, /device:TPU:21, one launch (start us, length us, event | category | flops | bytes accessed | tf_op | source)
XLA Modules:
  0.0 24.8 jit_solution(18119447217664090746)
XLA Ops:
  0.0 23.1 %shard_map.37 = bf16[128,1024]{1,0:T(8,128)(2,1)} custom-call(bf16[128,1024]{1,0:T(8,128)(2,1)} %bitcast.5, bf16[128,1024]{1,0:T(8,128)(2,1)} %bitcast.6, bf16[128,1024]{1,0:T(8,128)(2,1)} %bitcast.7), custom_call_target="tpu_custom_call" | custom-call | flops 268435456 | bytes 1048576 | tf_op jit(solution)/shard_map/pallas_call | solution.py:323
  23.1 1.7 %copy.5 = bf16[2,64,1024]{2,1,0:T(8,128)(2,1)} copy(bf16[2,64,1024]{2,1,0:T(8,128)(2,1)} %bitcast.4) | data formatting | bytes 524288

commit v3 on v2

--- a/solution.py
+++ b/solution.py
@@ -136,20 +136,15 @@
         push(item, start)
     for copy in loads:
         copy.wait()
-    sib_whole(start)
     for h in range(half):
         sib_push(h, start)
+    sib_whole(start)
 
     row_band = lax.broadcasted_iota(jnp.int32, (rows, rows), 0) // patches
     key_band = lax.broadcasted_iota(jnp.int32, (rows, rows), 1) // patches
     keep = row_band >= key_band
 
     keep2 = jnp.concatenate([keep, jnp.full((rows, rows), True)], axis=1)
-
-    @pl.when(c == 1)
-    def _():
-        for n, dst in enumerate((sib_k, sib_v)):
-            remote(dst, dst, sib_send.at[n], sib_recv.at[n], sib).wait_recv()
 
     def attend_local(h):
         at = lanes(h)
@@ -212,48 +207,53 @@
 
     for item in range(heads):
         h = item // 2
-        attend_local(item)
         if item + WINDOW < heads:
             push(item, wait_send)
             push(item + WINDOW, start)
-        if item % 2 == 1:
+        if item % 2 == 0:
             wait_local_kv(h)
             wait_own_q(h)
 
+            @pl.when(lower)
+            def _():
+                each(0, z, lambda i: wait_kv(i, h))
+
+                @pl.when(z == hub)
+                def _():
+                    def body(n):
+                        j = chips - 1 - n
+                        wait_q(j, h)
+                        compute(j - mid, h, 0, 2 * mid * rows, 0, j)
+                    each(0, chips - mid, body)
+
+                def body(i):
+                    o, s = block(mid, h, i * 2 * rows, 2 * rows)
+                    for cc in range(2):
+                        @pl.when(cc == c)
+                        def _():
+                            part[i, c * half + h] = o[cc * rows : (cc + 1) * rows]
+                            stat[i, c * half + h] = s[:, cc * rows : (cc + 1) * rows]
+
+                        @pl.when(cc != c)
+                        def _():
+                            out_p[mid + i, cc, h] = o[cc * rows : (cc + 1) * rows]
+                            out_s[mid + i, cc, h] = s[:, cc * rows : (cc + 1) * rows]
+                            deliver(mid + i, h, i, z, cc, start)
+                each(0, z, body)
+
+        if item == 0:
+            @pl.when(c == 1)
+            def _():
+                for n, dst in enumerate((sib_k, sib_v)):
+                    remote(dst, dst, sib_send.at[n], sib_recv.at[n], sib).wait_recv()
+        attend_local(item)
+        if item % 2 == 1:
             @pl.when(jnp.logical_not(lower))
             def _():
                 def body(j):
                     wait_q(j, h)
                     compute(j - mid, h, 0, 2 * rows, 1 + z - mid, j)
                 each(z + 1, chips, body)
-
-    for h in range(half):
-        @pl.when(lower)
-        def _():
-            each(0, z, lambda i: wait_kv(i, h))
-
-            @pl.when(z == hub)
-            def _():
-                def body(n):
-                    j = chips - 1 - n
-                    wait_q(j, h)
-                    compute(j - mid, h, 0, 2 * mid * rows, 0, j)
-                each(0, chips - mid, body)
-
-            def body(i):
-                o, s = block(mid, h, i * 2 * rows, 2 * rows)
-                for cc in range(2):
-                    @pl.when(cc == c)
-                    def _():
-                        part[i, c * half + h] = o[cc * rows : (cc + 1) * rows]
-                        stat[i, c * half + h] = s[:, cc * rows : (cc + 1) * rows]
-
-                    @pl.when(cc != c)
-                    def _():
-                        out_p[mid + i, cc, h] = o[cc * rows : (cc + 1) * rows]
-                        out_s[mid + i, cc, h] = s[:, cc * rows : (cc + 1) * rows]
-                        deliver(mid + i, h, i, z, cc, start)
-            each(0, z, body)
 
     def out_copy(head):
         at = lanes(head)

time: 24.9 us -> 24.5 us (0.984)
  Pallas kernels: 23.1 us -> 22.6 us
    pallas_call x1, Pallas kernels: 23.1 us -> 22.6 us  [shards(): pl.pallas_call(functools.partial(kernel, chips, patch_count), out_shape=j...]
where the time goes in v3:
time: 24.5 us; the launch traced here: 24.3 us
  Pallas kernels  22.6 us (92%)
  local copies, waits for them, and re-layouts  1.67 us (7%)
    pallas_call x1, Pallas kernels, shards(): pl.pallas_call(functools.partial(kernel, chips, patch_count), out_shape=j...  22.6 us
    unnamed x1, local copies, waits for them, and re-layouts  1.67 us

profile of v3, /device:TPU:21, one launch (start us, length us, event | category | flops | bytes accessed | tf_op | source)
XLA Modules:
  0.0 24.3 jit_solution(6080393765504304299)
XLA Ops:
  0.0 22.6 %shard_map.37 = bf16[128,1024]{1,0:T(8,128)(2,1)} custom-call(bf16[128,1024]{1,0:T(8,128)(2,1)} %bitcast.5, bf16[128,1024]{1,0:T(8,128)(2,1)} %bitcast.6, bf16[128,1024]{1,0:T(8,128)(2,1)} %bitcast.7), custom_call_target="tpu_custom_call" | custom-call | flops 268435456 | bytes 1048576 | tf_op jit(solution)/shard_map/pallas_call | solution.py:323
  22.6 1.7 %copy.5 = bf16[2,64,1024]{2,1,0:T(8,128)(2,1)} copy(bf16[2,64,1024]{2,1,0:T(8,128)(2,1)} %bitcast.4) | data formatting | bytes 524288

commit v4 on v3

--- a/solution.py
+++ b/solution.py
@@ -176,10 +176,13 @@
                       part_send.at[q_slot, cc, h, n], part_recv.at[slot, c * half + h, n], chip * 2 + cc))
 
     def compute(q_slot, h, key_at, key_count, slot, chip):
-        o, s = block(q_slot, h, key_at, key_count)
+        keys = pl.ds(key_at, key_count)
         for cc in range(2):
-            out_p[q_slot, cc, h] = o[cc * rows : (cc + 1) * rows]
-            out_s[q_slot, cc, h] = s[:, cc * rows : (cc + 1) * rows]
+            o, s = softmax_block(
+                qall[h, span((q_slot * 2 + cc) * rows), :], kall[h, keys, :], vall[h, keys, :]
+            )
+            out_p[q_slot, cc, h] = o.astype(jnp.bfloat16)
+            out_s[q_slot, cc, h] = s.T[0:1, :]
             deliver(q_slot, h, slot, chip, cc, start)
 
     def wait_local_kv(h):

time: 24.5 us -> 26.3 us (1.073)
  the two profiles are of different devices: /device:TPU:21 before, /device:TPU:15 now
where the time goes in v4:
time: 26.3 us; the launch traced here: 26.1 us
  Pallas kernels  24.5 us (93%)
  local copies, waits for them, and re-layouts  1.67 us (6%)
    pallas_call x1, Pallas kernels, shards(): pl.pallas_call(functools.partial(kernel, chips, patch_count), out_shape=j...  24.5 us
    unnamed x1, local copies, waits for them, and re-layouts  1.67 us

profile of v4, /device:TPU:15, one launch (start us, length us, event | category | flops | bytes accessed | tf_op | source)
XLA Modules:
  0.0 26.1 jit_solution(6402241437085922223)
XLA Ops:
  0.0 24.5 %shard_map.37 = bf16[128,1024]{1,0:T(8,128)(2,1)} custom-call(bf16[128,1024]{1,0:T(8,128)(2,1)} %bitcast.5, bf16[128,1024]{1,0:T(8,128)(2,1)} %bitcast.6, bf16[128,1024]{1,0:T(8,128)(2,1)} %bitcast.7), custom_call_target="tpu_custom_call" | custom-call | flops 268435456 | bytes 1048576 | tf_op jit(solution)/shard_map/pallas_call | solution.py:326
  24.5 1.7 %copy.5 = bf16[2,64,1024]{2,1,0:T(8,128)(2,1)} copy(bf16[2,64,1024]{2,1,0:T(8,128)(2,1)} %bitcast.4) | data formatting | bytes 524288

commit v5 on v3

--- a/solution.py
+++ b/solution.py
@@ -39,6 +39,8 @@
     half = heads // 2
     mid = chips // 2
     hub = mid - 1
+    upper = chips - mid
+    group = 2 if upper % 2 == 0 else 1
     me = lax.axis_index("blk")
     z, c = me // 2, me % 2
     other = 1 - c
@@ -221,10 +223,21 @@
                 @pl.when(z == hub)
                 def _():
                     def body(n):
-                        j = chips - 1 - n
-                        wait_q(j, h)
-                        compute(j - mid, h, 0, 2 * mid * rows, 0, j)
-                    each(0, chips - mid, body)
+                        first = (upper // group - 1 - n) * group
+                        for g in range(group):
+                            wait_q(mid + first + g, h)
+                        keys = 2 * mid * rows
+                        o, s = softmax_block(
+                            qall[h, span(first * 2 * rows, 2 * group), :], kall[h, 0:keys, :], vall[h, 0:keys, :]
+                        )
+                        o, s = o.astype(jnp.bfloat16), s.T[0:1, :]
+                        for g in reversed(range(group)):
+                            for cc in range(2):
+                                at = (g * 2 + cc) * rows
+                                out_p[first + g, cc, h] = o[at : at + rows]
+                                out_s[first + g, cc, h] = s[:, at : at + rows]
+                                deliver(first + g, h, 0, mid + first + g, cc, start)
+                    each(0, upper // group, body)
 
                 def body(i):
                     o, s = block(mid, h, i * 2 * rows, 2 * rows)

time: 24.5 us -> 25.6 us (1.045)
  Pallas kernels: 22.6 us -> 23.8 us
    pallas_call x1, Pallas kernels: 22.6 us -> 23.8 us  [shards(): pl.pallas_call(functools.partial(kernel, chips, patch_count), out_shape=j...]
where the time goes in v5:
time: 25.6 us; the launch traced here: 25.5 us
  Pallas kernels  23.8 us (93%)
  local copies, waits for them, and re-layouts  1.67 us (7%)
    pallas_call x1, Pallas kernels, shards(): pl.pallas_call(functools.partial(kernel, chips, patch_count), out_shape=j...  23.8 us
    unnamed x1, local copies, waits for them, and re-layouts  1.67 us

profile of v5, /device:TPU:21, one launch (start us, length us, event | category | flops | bytes accessed | tf_op | source)
XLA Modules:
  0.0 25.5 jit_solution(9005163724788670610)
XLA Ops:
  0.0 23.8 %shard_map.37 = bf16[128,1024]{1,0:T(8,128)(2,1)} custom-call(bf16[128,1024]{1,0:T(8,128)(2,1)} %bitcast.5, bf16[128,1024]{1,0:T(8,128)(2,1)} %bitcast.6, bf16[128,1024]{1,0:T(8,128)(2,1)} %bitcast.7), custom_call_target="tpu_custom_call" | custom-call | flops 268435456 | bytes 1048576 | tf_op jit(solution)/shard_map/pallas_call | solution.py:336
  23.8 1.7 %copy.5 = bf16[2,64,1024]{2,1,0:T(8,128)(2,1)} copy(bf16[2,64,1024]{2,1,0:T(8,128)(2,1)} %bitcast.4) | data formatting | bytes 524288
